TPU v7x, 32 devices: a whole 2x2x4 slice. The times are simulated.
32 devices in a mesh: row: 8 (over z, y), col: 4 (over x, core).
Axes of the slice: x: 2, y: 2, z: 4, core: 2. Of those that a mesh axis runs over, the one named last changes fastest.
Arguments:
- design: bfloat16 [5120, 8192], P('row', 'col'), may hold values from -0.125 to 0.125
- projector: bfloat16 [4, 5120, 640], P('col', 'row')
- targets: float32 [5120], P('row'), may hold values from -6 to 6
- sparsity: float32 [32], replicated, may hold values from 0.02 to 0.6
- ridge_weight: float32 [32], replicated, may hold values from 0.05 to 2
- coefficients: float32 [32, 8192], P(None, 'col'), may hold values from -4 to 4
- block_duals: float32 [8, 32, 8192], P('row', None, 'col'), may hold values from -4 to 4
- row_duals: float32 [32, 5120], P(None, 'row'), may hold values from -3 to 3
- block_fits: float32 [4, 32, 5120], P('col', None, 'row'), may hold values from -3 to 3
Outputs:
- estimate: float32 [32, 8192], P(None, 'col')
- column_duals: float32 [32, 8192], P(None, 'col')
- next_block_duals: float32 [8, 32, 8192], P('row', None, 'col')
- next_row_duals: float32 [32, 5120], P(None, 'row')
All inputs are finite; a program needn't handle non-finite values.
Results may differ from a plain program's by a relative error of at most 0.013.
Values sent between devices are 32-bit elements; how exact they have to be, the bound alone decides.
A program may use at most 64 MiB of HBM per device.

v0:
```python
import jax
import jax.numpy as jnp
from jax import lax
from jax.sharding import PartitionSpec as P

ITERS = 5


def shrink(values, threshold):
    return jnp.maximum(values - threshold, 0.0) - jnp.maximum(-values - threshold, 0.0)


def times_transpose(left, design):
    return lax.dot_general(
        left, design, (((1,), (1,)), ((), ())), preferred_element_type=jnp.float32
    )


def per_device(
    design,
    projector,
    targets,
    sparsity,
    ridge_weight,
    coefficients,
    block_duals,
    row_duals,
    block_fits,
):
    row_count = lax.axis_size("row")
    col_count = lax.axis_size("col")
    inverse = projector[0]
    shares = block_duals[0]
    fits = block_fits[0]
    threshold = sparsity[:, None]
    shrink_by = 1.0 / (1.0 + ridge_weight[:, None])
    current = coefficients
    duals_row = row_duals
    column_dual = -lax.psum(shares, "row")
    row_fit = lax.psum(fits, "col")
    for iteration in range(ITERS):
        duals_part = duals_row
        half_row = 0.5 * (row_fit - duals_part + targets[None, :])
        current_part = current
        half_col = shrink(current_part - column_dual, threshold) * shrink_by
        lifted = (fits + duals_row).astype(jnp.bfloat16)
        start = current - shares + jnp.dot(lifted, design, preferred_element_type=jnp.float32)
        image = times_transpose(start.astype(jnp.bfloat16), design)
        weighted = jnp.dot(image.astype(jnp.bfloat16), inverse, preferred_element_type=jnp.float32)
        block_x = start - jnp.dot(
            weighted.astype(jnp.bfloat16), design, preferred_element_type=jnp.float32
        )
        block_y = times_transpose(block_x.astype(jnp.bfloat16), design)
        total = lax.psum(block_x, "row")
        average = (half_col + total) / (row_count + 1)
        column_dual = column_dual + half_col - average
        shares = shares + block_x - average
        fitted = lax.psum(block_y, "col")
        misfit = (half_row - fitted) / (col_count + 1)
        row_fit = half_row - misfit
        fits = block_y + misfit
        duals_row = duals_row + misfit
        current = average
    return (current, column_dual, shares[None], duals_row)


def solution(mesh):
    return jax.shard_map(
        per_device,
        mesh=mesh,
        in_specs=(
            P("row", "col"),
            P("col", "row", None),
            P("row"),
            P(),
            P(),
            P(None, "col"),
            P("row", None, "col"),
            P(None, "row"),
            P("col", None, "row"),
        ),
        out_specs=(P(None, "col"), P(None, "col"), P("row", None, "col"), P(None, "row")),
        check_vma=False,
    )
```

profile of v0, /device:TPU:0, one launch (start us, length us, event | category | flops | bytes accessed | tf_op | source)
XLA Modules:
  0.0 589.1 jit_solution(16335704082272334949)
XLA Ops:
  7.2 1.7 copy-done
  8.9 2.4 convolution_add_fusion.4
  11.3 2.2 convolution_convert_fusion.8
  13.5 1.5 convolution_subtract_fusion.4
  15.0 0.7 copy-done.3
  15.7 1.5 fusion.21
  17.3 0.7 all-reduce.29.cloned.1.call-update
  18.1 33.7 %all-reduce.31.cloned.1.call-done = (f32[32,640]{1,0:T(8,128)}, f32[32,640]{1,0:T(8,128)}) async-done(((f32[32,640]{1,0:T(8,128)}, f32[32,640]{1,0:T(8,128)}), (f32[32,640]{1,0:T(8,128)}, f32[32,640]{1,0:T(8,128)})) %all-reduce.31.cloned.1.call-update) | async-done | bytes 163856 | tf_op jit(solution)/shard_map/psum | solution.py:58
  51.8 1.6 add_multiply_fusion.7
  53.4 75.5 %all-reduce.29.cloned.1.call-done = (f32[32,2048]{1,0:T(8,128)}, f32[32,2048]{1,0:T(8,128)}) async-done(((f32[32,2048]{1,0:T(8,128)}, f32[32,2048]{1,0:T(8,128)}), (f32[32,2048]{1,0:T(8,128)}, f32[32,2048]{1,0:T(8,128)})) %all-reduce.29.cloned.1.call-update) | async-done | bytes 524304 | tf_op jit(solution)/shard_map/psum | solution.py:54
  128.9 2.7 convolution_add_fusion.3
  131.6 2.8 convolution_convert_fusion.6
  134.4 2.2 convolution_subtract_fusion.3
  136.6 0.0 all-reduce.15.cloned.1.call-start
  136.7 2.5 fusion.17
  139.2 0.0 all-reduce.17.cloned.1.call-start
  139.2 67.3 %all-reduce.13.cloned.1.call-done = f32[32,2048]{1,0:T(8,128)} async-done(((f32[32,2048]{1,0:T(8,128)}), f32[32,2048]{1,0:T(8,128)}) %all-reduce.13.cloned.1.call-update) | async-done | bytes 262160 | tf_op jit(solution)/shard_map/psum | solution.py:54
  206.6 2.5 add_subtract_fusion.5
  209.1 29.4 %all-reduce.15.cloned.1.call-done = f32[32,640]{1,0:T(8,128)} async-done(((f32[32,640]{1,0:T(8,128)}), f32[32,640]{1,0:T(8,128)}) %all-reduce.15.cloned.1.call-update) | async-done | bytes 81936 | tf_op jit(solution)/shard_map/psum | solution.py:58
  238.5 2.4 convolution_add_fusion.2
  240.9 2.8 convolution_convert_fusion.4
  243.7 2.2 convolution_subtract_fusion.2
  245.9 0.0 all-reduce.19.cloned.1.call-start
  246.0 2.5 fusion.13
  248.5 0.0 all-reduce.21.cloned.1.call-start
  248.5 69.6 %all-reduce.17.cloned.1.call-done = f32[32,2048]{1,0:T(8,128)} async-done(((f32[32,2048]{1,0:T(8,128)}), f32[32,2048]{1,0:T(8,128)}) %all-reduce.17.cloned.1.call-update) | async-done | bytes 262160 | tf_op jit(solution)/shard_map/psum | solution.py:54
  318.1 2.4 add_multiply_fusion.2
  320.5 29.5 %all-reduce.19.cloned.1.call-done = f32[32,640]{1,0:T(8,128)} async-done(((f32[32,640]{1,0:T(8,128)}), f32[32,640]{1,0:T(8,128)}) %all-reduce.19.cloned.1.call-update) | async-done | bytes 81936 | tf_op jit(solution)/shard_map/psum | solution.py:58
  350.0 2.5 convolution_add_fusion.1
  352.6 2.8 convolution_convert_fusion.2
  355.4 2.2 convolution_subtract_fusion.1
  357.6 0.0 all-reduce.23.cloned.1.call-start
  357.7 2.5 fusion.9
  360.2 0.0 all-reduce.27.cloned.1.call-start
  360.2 69.6 %all-reduce.21.cloned.1.call-done = f32[32,2048]{1,0:T(8,128)} async-done(((f32[32,2048]{1,0:T(8,128)}), f32[32,2048]{1,0:T(8,128)}) %all-reduce.21.cloned.1.call-update) | async-done | bytes 262160 | tf_op jit(solution)/shard_map/psum | solution.py:54
  429.9 2.5 add_subtract_fusion.1
  432.4 29.6 %all-reduce.23.cloned.1.call-done = f32[32,640]{1,0:T(8,128)} async-done(((f32[32,640]{1,0:T(8,128)}), f32[32,640]{1,0:T(8,128)}) %all-reduce.23.cloned.1.call-update) | async-done | bytes 81936 | tf_op jit(solution)/shard_map/psum | solution.py:58
  461.9 2.5 convolution_add_fusion
  464.4 2.8 convolution_convert_fusion
  467.2 1.5 convolution_subtract_fusion
  468.8 1.5 fusion.5
  470.3 0.0 all-reduce.25.cloned.1.call-start
  470.4 0.5 all-reduce.25.cloned.1.call-update
  470.9 30.8 %all-reduce.27.cloned.1.call-done = f32[32,640]{1,0:T(8,128)} async-done(((f32[32,640]{1,0:T(8,128)}), f32[32,640]{1,0:T(8,128)}) %all-reduce.27.cloned.1.call-update) | async-done | bytes 81936 | tf_op jit(solution)/shard_map/psum | solution.py:58
  501.7 1.8 multiply_add_fusion
  503.5 74.4 %all-reduce.25.cloned.1.call-done = f32[32,2048]{1,0:T(8,128)} async-done(((f32[32,2048]{1,0:T(8,128)}), f32[32,2048]{1,0:T(8,128)}) %all-reduce.25.cloned.1.call-update) | async-done | bytes 262160 | tf_op jit(solution)/shard_map/psum | solution.py:54
  577.9 2.3 subtract_bitcast_fusion
  580.2 2.1 add_subtract_fusion
  (32 shorter events, 0.3 us)
Async XLA Ops:
  7.2 1.7 copy-start
  7.2 4.1 copy-start.1
  7.2 44.6 %all-reduce.31.cloned.1.call-start = ((), (), s32[]{:S(2)}) async-start(), calls=%async_computation.9 | async-start | bytes 327680 | tf_op jit(solution)/shard_map/psum | solution.py:58
  15.0 0.7 copy-start.3
  15.7 2.4 copy-start.10
  15.7 36.1 %copy-start.8 = (f32[640]{0:T(1024)S(1)}, f32[640]{0:T(1024)}, u32[]{:S(2)}) copy-start(f32[640]{0:T(1024)} %param.11) | copy-start | bytes 7684
  15.7 113.2 %copy-start.9 = (f32[32]{0:T(128)S(1)}, f32[32]{0:T(128)}, u32[]{:S(2)}) copy-start(f32[32]{0:T(128)} %param.12) | copy-start | bytes 388
  17.3 111.6 %all-reduce.29.cloned.1.call-start = ((), (), s32[]{:S(2)}) async-start(), calls=%async_computation.8 | async-start | bytes 1048576 | tf_op jit(solution)/shard_map/psum | solution.py:54
  18.0 188.6 %all-reduce.13.cloned.1.call-start = ((), (), s32[]{:S(2)}) async-start(), calls=%async_computation | async-start | bytes 524288 | tf_op jit(solution)/shard_map/psum | solution.py:54
  136.6 101.8 %all-reduce.15.cloned.1.call-start = ((), (), s32[]{:S(2)}) async-start(), calls=%async_computation.1 | async-start | bytes 163840 | tf_op jit(solution)/shard_map/psum | solution.py:58
  139.2 179.0 %all-reduce.17.cloned.1.call-start = ((), (), s32[]{:S(2)}) async-start(), calls=%async_computation.2 | async-start | bytes 524288 | tf_op jit(solution)/shard_map/psum | solution.py:54
  245.9 104.1 %all-reduce.19.cloned.1.call-start = ((), (), s32[]{:S(2)}) async-start(), calls=%async_computation.3 | async-start | bytes 163840 | tf_op jit(solution)/shard_map/psum | solution.py:58
  248.5 181.4 %all-reduce.21.cloned.1.call-start = ((), (), s32[]{:S(2)}) async-start(), calls=%async_computation.4 | async-start | bytes 524288 | tf_op jit(solution)/shard_map/psum | solution.py:54
  357.6 104.3 %all-reduce.23.cloned.1.call-start = ((), (), s32[]{:S(2)}) async-start(), calls=%async_computation.5 | async-start | bytes 163840 | tf_op jit(solution)/shard_map/psum | solution.py:58
  360.2 141.5 %all-reduce.27.cloned.1.call-start = ((), (), s32[]{:S(2)}) async-start(), calls=%async_computation.7 | async-start | bytes 163840 | tf_op jit(solution)/shard_map/psum | solution.py:58
  468.7 1.6 copy-start.5
  468.8 109.1 %copy-start.2 = (f32[32,2048]{1,0:T(8,128)S(1)}, f32[32,2048]{1,0:T(8,128)}, u32[]{:S(2)}) copy-start(f32[32,2048]{1,0:T(8,128)} %get-tuple-element.17) | copy-start | bytes 786436
  468.8 109.1 %copy-start.4 = (f32[32,2048]{1,0:T(8,128)S(1)}, f32[32,2048]{1,0:T(8,128)}, u32[]{:S(2)}) copy-start(f32[32,2048]{1,0:T(8,128)} %get-tuple-element.12) | copy-start | bytes 786436
  470.3 107.6 %all-reduce.25.cloned.1.call-start = ((), (), s32[]{:S(2)}) async-start(), calls=%async_computation.6 | async-start | bytes 524288 | tf_op jit(solution)/shard_map/psum | solution.py:54
  470.9 109.3 %copy-start.6 = (f32[32,2048]{1,0:T(8,128)S(1)}, f32[32,2048]{1,0:T(8,128)}, u32[]{:S(2)}) copy-start(f32[32,2048]{1,0:T(8,128)} %get-tuple-element.13) | copy-start | bytes 786436
  580.2 2.1 copy-start.7
Sparse Core Ops, SparseCore 0:
  17.4 34.3 all-reduce.30
  56.2 72.6 all-reduce.28
  136.8 69.7 all-reduce.12
  209.4 28.9 all-reduce.14
  246.1 72.0 all-reduce.16
  321.0 28.9 all-reduce.18
  357.8 72.0 all-reduce.20
  432.9 28.9 all-reduce.22
  470.4 31.2 all-reduce.26
  505.8 72.0 all-reduce.24
where the time goes:
time: 590 us; the launch traced here: 589 us
  waiting for transfers between devices  511 us (87%)
  matrix products  46.1 us (8%)
  other arithmetic  15.2 us (3%)
  between operations  14.3 us (2%)
    psum x5, waiting for transfers between devices, per_device(): total = lax.psum(block_x, 'row')  356 us
    psum x5, waiting for transfers between devices, per_device(): fitted = lax.psum(block_y, 'col')  153 us
    dot_general x5, matrix products, per_device(): jnp.dot(image.astype(jnp.bfloat16), inverse, preferred_element_type=jnp.f...  13.4 us
    dot_general x5, matrix products, per_device(): jnp.dot(lifted, design, preferred_element_type=jnp.float32)  12.5 us
  transfers between devices with their start and end apart: 10, of which 10 were waited for; matrix products, arithmetic and copies ran while one was open for 3% of the time, Pallas kernels for 0%

commit v1 on v0

v1 whole, which is shorter than its diff:
```python
import functools

import jax
import jax.numpy as jnp
from jax import lax
from jax.experimental import pallas as pl
from jax.experimental.pallas import tpu as pltpu
from jax.sharding import PartitionSpec as P

ITERS = 5
MESH = pl.DeviceIdType.MESH
BF16 = jnp.bfloat16
F32 = jnp.float32


def shrink(values, threshold):
    return jnp.maximum(values - threshold, 0.0) - jnp.maximum(-values - threshold, 0.0)


def times(left, right):
    return jnp.dot(left, right, preferred_element_type=F32)


def times_transpose(left, right):
    return lax.dot_general(left, right, (((1,), (1,)), ((), ())), preferred_element_type=F32)


def kernel(
    rows, cols, split,
    design, projector, targets, sparsity, ridge, coefficients, block_duals, row_duals, block_fits,
    o_z, o_xc, o_xd, o_yd,
    A, K, S, XD, PX, AV, XB, PY, FIT, YD, YR, U, THR, SHR, XC, HC,
    R1, T1, R2, Q1, G1, Q2,
    load_a, load_k, load_v, load_x, load_z, store,
    s1_send, s1_recv, s2_send, s2_recv, q1_send, q1_recv, q2_send, q2_recv,
    z_send, z_recv, y_send, y_recv, bz_send, bz_recv, by_send, by_recv, p_send, p_recv,
):
    depth = rows // 2
    blocks, size, width = S.shape
    part = size // split
    me_row, me_col = lax.axis_index("row"), lax.axis_index("col")
    hi, lo = me_row // 2, me_row % 2
    pair = {"row": 2 * hi + 1 - lo}

    def near(k):
        return lax.rem(hi + k + depth, depth)

    def line(k):
        return {"row": 2 * near(k) + lo}

    def beside(k):
        return {"col": lax.rem(me_col + k, cols)}

    def block_of(p):
        return p // split

    def piece(ref, p):
        if split == 1:
            return ref.at[p]
        return ref.at[p // split, pl.ds(pl.multiple_of((p % split) * part, part), part), :]

    def remote(src, dst, send, recv, device):
        return pltpu.make_async_remote_copy(
            src_ref=src, dst_ref=dst, send_sem=send, recv_sem=recv, device_id=device, device_id_type=MESH)

    def columns(c):
        return pl.ds(c * width, width)

    order = list(range(1, depth)) + [0]

    barrier = pltpu.get_barrier_semaphore()
    peers = [pair] + [line(k) for k in range(1, depth)] + [beside(k) for k in range(1, cols)]
    for peer in peers:
        pl.semaphore_signal(barrier, inc=1, device_id=peer, device_id_type=MESH)

    load_xd = [pltpu.make_async_copy(block_duals.at[0, :, columns(c)], XD.at[c], load_x.at[c]) for c in range(blocks)]
    load_fit = pltpu.make_async_copy(block_fits.at[0], FIT, load_v.at[0])
    load_yd = pltpu.make_async_copy(row_duals, YD, load_v.at[1])
    load_zs = [pltpu.make_async_copy(coefficients.at[:, columns(c)], AV.at[c], load_z.at[c]) for c in range(blocks)]
    load_as = [pltpu.make_async_copy(design.at[:, columns(c)], A.at[c], load_a.at[c]) for c in range(blocks)]
    load_kk = pltpu.make_async_copy(projector.at[0], K, load_k.at[0])
    for copy in load_xd + [load_fit, load_yd]:
        copy.start()
    for c in range(blocks):
        load_as[c].start()
        load_zs[c].start()
    load_kk.start()

    eye = lax.broadcasted_iota(jnp.int32, (size, size), 0) == lax.broadcasted_iota(jnp.int32, (size, size), 1)

    def upright(ref):
        return jnp.sum(jnp.where(eye, ref[...], 0.0), axis=1, keepdims=True)

    THR[...] = jnp.broadcast_to(upright(sparsity), (size, width))
    SHR[...] = jnp.broadcast_to(1.0 / (1.0 + upright(ridge)), (size, width))

    pl.semaphore_wait(barrier, len(peers))

    for copy in load_xd:
        copy.wait()
    first = {}
    for k in order:
        first[k] = remote(piece(XD, 2 * near(k) + 1 - lo), Q1.at[k], q1_send.at[k], q1_recv.at[k], pair)
        first[k].start()
    load_fit.wait()
    load_yd.wait()

    def send_fit(slot, k):
        return remote(PY.at[slot, me_col], PY.at[slot, me_col], p_send.at[slot, k - 1], p_recv.at[slot, k - 1], beside(k))

    def take_fit(slot, k):
        source = lax.rem(me_col + cols - k, cols)
        remote(PY.at[slot, source], PY.at[slot, source], p_send.at[slot, k - 1], p_recv.at[slot, k - 1], beside(k)).wait_recv()

    def sum_fit(slot):
        total = PY[slot, 0]
        for j in range(1, cols):
            total = total + PY[slot, j]
        return total

    PY[2, me_col] = FIT[...]
    for k in range(1, cols):
        send_fit(2, k).start()

    lifted = (FIT[...] + YD[...]).astype(BF16)
    total_u = None
    for c in range(blocks):
        load_as[c].wait()
        load_zs[c].wait()
        s = AV[c] - XD[c] + times(lifted, A[c])
        S[c] = s
        u = times_transpose(s.astype(BF16), A[c])
        total_u = u if total_u is None else total_u + u
    U[...] = total_u

    for k in order:
        first[k].wait_recv()
        G1[k] = piece(XD, 2 * near(k) + lo)[...] + Q1[k]
        if k:
            remote(G1.at[k], Q2.at[k - 1], q2_send.at[k - 1], q2_recv.at[k - 1], line(k)).start()
    load_kk.wait()

    def stage_one(k):
        return remote(piece(PX, 2 * near(k) + 1 - lo), R1.at[k], s1_send.at[k], s1_recv.at[k], pair)

    def stage_two(k):
        return remote(T1.at[k], R2.at[k - 1], s2_send.at[k - 1], s2_recv.at[k - 1], line(k))

    def spread_line(ref, send, recv, k):
        mine = piece(ref, me_row)
        return remote(mine, mine, send.at[k - 1], recv.at[k - 1], line(k))

    def take_line(ref, send, recv, k):
        other = piece(ref, 2 * near(-k) + lo)
        remote(other, other, send.at[k - 1], recv.at[k - 1], line(k)).wait_recv()

    def spread_pair(ref, send, recv, k):
        other = piece(ref, 2 * near(-k) + lo)
        return remote(other, other, send.at[k], recv.at[k], pair)

    def take_pair(ref, send, recv, k):
        other = piece(ref, 2 * near(-k) + 1 - lo)
        remote(other, other, send.at[k], recv.at[k], pair).wait_recv()

    def project(slot):
        w = times(U[...].astype(BF16), K[...]).astype(BF16)

        def block_x(c):
            PX[c] = S[c] - times(w, A[c])

        for k in order:
            block_x(block_of(2 * near(k) + 1 - lo))
            stage_one(k).start()
        if split == 1:
            for k in order:
                block_x(2 * near(k) + lo)
        block_y = None
        for c in range(blocks):
            y = times_transpose(PX[c].astype(BF16), A[c])
            block_y = y if block_y is None else block_y + y
        PY[slot, me_col] = block_y
        for k in range(1, cols):
            send_fit(slot, k).start()
        for k in order:
            stage_one(k).wait_recv()
            T1[k] = piece(PX, 2 * near(k) + lo)[...] + R1[k]
            if k:
                stage_two(k).start()

    my_rows = pl.ds(pl.multiple_of((me_row % split) * part, part), part)

    def half_col():
        return shrink(piece(AV, me_row)[...] - XC[...], THR[my_rows, :]) * SHR[my_rows, :]

    def average():
        total = T1[0]
        for k in range(1, depth):
            stage_two(k).wait_recv()
            total = total + R2[k - 1]
        avg = (HC[...] + total) / (rows + 1)
        piece(AV, me_row)[...] = avg
        for k in range(1, depth):
            spread_line(AV, z_send, z_recv, k).start()
        spread_pair(AV, y_send, y_recv, 0).start()
        return avg

    def row_update(slot):
        half_row = 0.5 * (YR[...] - YD[...] + targets[...])
        for k in range(1, cols):
            take_fit(slot, k)
        misfit = (half_row - sum_fit(slot)) / (cols + 1)
        YR[...] = half_row - misfit
        YD[...] = YD[...] + misfit
        return misfit

    def settle(slot):
        for k in order:
            stage_one(k).wait_send()
            if k:
                stage_two(k).wait_send()
                spread_line(AV, z_send, z_recv, k).wait_send()
            spread_pair(AV, y_send, y_recv, k).wait_send()
        for k in range(1, cols):
            send_fit(slot, k).wait_send()

    def relay(ref, send, recv, pair_send, pair_recv):
        for k in range(1, depth):
            take_line(ref, send, recv, k)
            spread_pair(ref, pair_send, pair_recv, k).start()

    project(0)

    total = G1[0]
    for k in range(1, depth):
        remote(G1.at[k], Q2.at[k - 1], q2_send.at[k - 1], q2_recv.at[k - 1], line(k)).wait_recv()
        total = total + Q2[k - 1]
    XC[...] = -total
    HC[...] = half_col()
    for k in range(1, cols):
        take_fit(2, k)
    YR[...] = sum_fit(2)
    for k in range(1, cols):
        send_fit(2, k).wait_send()
    for k in order:
        first[k].wait_send()
        if k:
            remote(G1.at[k], Q2.at[k - 1], q2_send.at[k - 1], q2_recv.at[k - 1], line(k)).wait_send()

    def step(t, carry):
        slot = lax.rem(t, 2)
        avg = average()
        XC[...] = XC[...] + HC[...] - avg
        HC[...] = half_col()
        misfit = row_update(slot)
        lifted = (PY[slot, me_col] + misfit + YD[...]).astype(BF16)
        for c in range(blocks):
            S[c] = times(lifted, A[c])

        def arrived(p):
            c = block_of(p)
            duals = XD[c] + PX[c] - AV[c]
            XD[c] = duals
            s = AV[c] - duals + S[c]
            S[c] = s
            return times_transpose(s.astype(BF16), A[c])

        relay(AV, z_send, z_recv, y_send, y_recv)
        total_u = jnp.zeros(U.shape, F32)
        if split == 1:
            for k in range(depth):
                total_u = total_u + arrived(2 * near(-k) + lo)
        for k in range(depth):
            take_pair(AV, y_send, y_recv, k)
            total_u = total_u + arrived(2 * near(-k) + 1 - lo)
        U[...] = total_u
        settle(slot)
        project(1 - slot)
        return carry

    lax.fori_loop(0, ITERS - 1, step, 0)

    slot = (ITERS - 1) % 2
    piece(XB, me_row)[...] = XC[...] + HC[...]
    for k in range(1, depth):
        spread_line(XB, bz_send, bz_recv, k).start()
    spread_pair(XB, by_send, by_recv, 0).start()
    average()
    relay(XB, bz_send, bz_recv, by_send, by_recv)
    row_update(slot)
    stores = [pltpu.make_async_copy(YD, o_yd, store.at[0, 0])]
    stores[0].start()
    relay(AV, z_send, z_recv, y_send, y_recv)

    def finish(p):
        c = block_of(p)
        where = pl.ds(pl.multiple_of(c * width, width), width)
        XD[c] = XD[c] + PX[c] - AV[c]
        XB[c] = XB[c] - AV[c]
        n = len(stores)
        for ref, out in ((AV, o_z), (XB, o_xc), (XD, o_xd.at[0])):
            copy = pltpu.make_async_copy(ref.at[c], out.at[:, where], store.at[n, len(stores) - n])
            copy.start()
            stores.append(copy)

    for k in range(depth):
        spread_pair(XB, by_send, by_recv, k).wait_send()
        if k:
            spread_line(XB, bz_send, bz_recv, k).wait_send()
    if split == 1:
        for k in range(depth):
            finish(2 * near(-k) + lo)
    for k in range(depth):
        take_pair(XB, by_send, by_recv, k)
        take_pair(AV, y_send, y_recv, k)
        finish(2 * near(-k) + 1 - lo)
    settle(slot)
    for copy in stores:
        copy.wait()


def per_device(design, projector, targets, sparsity, ridge_weight, coefficients, block_duals, row_duals, block_fits):
    rows, cols = lax.axis_size("row"), lax.axis_size("col")
    size, n = coefficients.shape
    m = design.shape[0]
    width = max(128, n // rows)
    blocks = n // width
    split = rows // blocks
    part, depth = size // split, rows // 2
    any_space = pl.BlockSpec(memory_space=pl.ANY)
    vmem = pl.BlockSpec(memory_space=pltpu.VMEM)
    dma = pltpu.SemaphoreType.DMA
    wide = pltpu.VMEM((blocks, size, width), F32)
    tall = pltpu.VMEM((size, m), F32)
    own = pltpu.VMEM((part, width), F32)

    def pieces(count):
        return pltpu.VMEM((count, part, width), F32)

    scratch = [
        pltpu.VMEM((blocks, m, width), BF16), pltpu.VMEM((m, m), BF16),
        wide, wide, wide, wide, wide,
        pltpu.VMEM((3, cols, size, m), F32), tall, tall, tall, tall,
        pltpu.VMEM((size, width), F32), pltpu.VMEM((size, width), F32), own, own,
        pieces(depth), pieces(depth), pieces(depth - 1), pieces(depth), pieces(depth), pieces(depth - 1),
        dma((blocks,)), dma((1,)), dma((2,)), dma((blocks,)), dma((blocks,)), dma((3 * blocks + 1, 3)),
        dma((depth,)), dma((depth,)), dma((depth - 1,)), dma((depth - 1,)),
        dma((depth,)), dma((depth,)), dma((depth - 1,)), dma((depth - 1,)),
        dma((depth - 1,)), dma((depth - 1,)), dma((depth,)), dma((depth,)),
        dma((depth - 1,)), dma((depth - 1,)), dma((depth,)), dma((depth,)),
        dma((3, cols - 1)), dma((3, cols - 1)),
    ]
    return pl.pallas_call(
        functools.partial(kernel, rows, cols, split),
        out_shape=(
            jax.ShapeDtypeStruct((size, n), F32),
            jax.ShapeDtypeStruct((size, n), F32),
            jax.ShapeDtypeStruct((1, size, n), F32),
            jax.ShapeDtypeStruct((size, m), F32),
        ),
        in_specs=[any_space, any_space, vmem, vmem, vmem, any_space, any_space, any_space, any_space],
        out_specs=[any_space] * 4,
        scratch_shapes=scratch,
        compiler_params=pltpu.CompilerParams(
            collective_id=0, has_side_effects=True, vmem_limit_bytes=40 * 1024 * 1024),
        name="admm",
    )(design, projector, targets.reshape(1, m), sparsity.reshape(1, size), ridge_weight.reshape(1, size),
      coefficients, block_duals, row_duals, block_fits)


def solution(mesh):
    return jax.shard_map(
        per_device,
        mesh=mesh,
        in_specs=(
            P("row", "col"),
            P("col", "row", None),
            P("row"),
            P(),
            P(),
            P(None, "col"),
            P("row", None, "col"),
            P(None, "row"),
            P("col", None, "row"),
        ),
        out_specs=(P(None, "col"), P(None, "col"), P("row", None, "col"), P(None, "row")),
        check_vma=False,
    )
```

time: 590 us -> 104 us (0.18)
  waiting for transfers between devices: 511 us -> 0 us
  Pallas kernels: 0 us -> 91.3 us
  matrix products: 46.1 us -> 0 us
  other arithmetic: 15.2 us -> 0 us
  between operations: 14.3 us -> 0.65 us
  local copies, waits for them, and re-layouts: 2.42 us -> 11.3 us
    psum x10 -> x0, waiting for transfers between devices: 509 us -> none  [the longest x5 356 us: per_device(): total = lax.psum(block_x, 'row')]
    pallas_call x0 -> x1, Pallas kernels: none -> 91.3 us  [per_device(): pl.pallas_call(functools.partial(kernel, rows, cols, split), out_shape=(j...]
    dot_general x20 -> x0, matrix products: 46.1 us -> none  [the longest x5 13.4 us: per_device(): jnp.dot(image.astype(jnp.bfloat16), inverse, preferred_element_type=jnp.f...]
    unnamed x22 -> x20, local copies, waits for them, and re-layouts: 2.42 us -> 10.6 us
    sub x3 -> x0, other arithmetic: 7.06 us -> none  [the longest x2 4.99 us: per_device(): shares = shares + block_x - average]
  transfers between devices with their start and end apart: 10 -> 0, of which waited for: 10 -> 0; matrix products, arithmetic and copies ran while one was open for 3% -> 0% of each run, Pallas kernels for 0% -> 0%
where the time goes in v1:
time: 104 us; the launch traced here: 103 us
  Pallas kernels  91.3 us (88%)
  local copies, waits for them, and re-layouts  11.3 us (11%)
    pallas_call x1, Pallas kernels, per_device(): pl.pallas_call(functools.partial(kernel, rows, cols, split), out_shape=(j...  91.3 us
    unnamed x20, local copies, waits for them, and re-layouts  10.6 us

profile of v1, /device:TPU:0, one launch (start us, length us, event | category | flops | bytes accessed | tf_op | source)
XLA Modules:
  0.0 103.2 jit_solution(2670451372075584764)
XLA Ops:
  0.6 0.7 reshape.17.targets
  1.3 0.0 copy-start
  1.3 1.7 %copy-done = bf16[640,2048]{1,0:T(8,128)(2,1)S(1)} copy-done((bf16[640,2048]{1,0:T(8,128)(2,1)S(1)}, bf16[640,2048]{1,0:T(8,128)(2,1)}, u32[]{:S(2)}) %copy-start) | copy-done | bytes 2621464
  3.1 0.0 copy-start.1
  3.1 1.1 %copy-done.1 = bf16[1,640,640]{2,1,0:T(8,128)(2,1)S(1)} copy-done((bf16[1,640,640]{2,1,0:T(8,128)(2,1)S(1)}, bf16[1,640,640]{2,1,0:T(8,128)(2,1)}, u32[]{:S(2)}) %copy-start.1) | copy-done | bytes 819224
  4.2 0.0 copy-start.2
  4.2 0.9 copy-done.2
  5.2 0.0 copy-start.3
  5.2 0.9 copy-done.3
  6.1 0.0 copy-start.4
  6.1 0.9 copy-done.4
  7.0 0.0 copy-start.5
  7.0 0.9 copy-done.5
  7.9 0.0 copy-start.6
  7.9 0.7 copy-done.6
  8.5 0.0 copy-start.7
  8.5 0.7 copy-done.7
  9.2 91.3 %admm.1 = (f32[32,2048]{1,0:T(8,128)S(1)}, f32[32,2048]{1,0:T(8,128)S(1)}, f32[1,32,2048]{2,1,0:T(8,128)S(1)}, f32[32,640]{1,0:T(8,128)S(1)}) custom-call(bf16[640,2048]{1,0:T(8,128)(2,1)S(1)} %copy-done, bf16[1,640,640]{2,1,0:T(8,128)(2,1)S(1)} %copy-done.1, f32[1,640]{1,0:T(1,128)S(1)} %reshape.17.targets, f32[1,32]{1,0:T(1,128)S(1)} %bitcast.2, ...), custom_call_target="tpu_custom_call" | custom-call | tf_op jit(solution)/shard_map/admm/pallas_call | solution.py:352
  100.5 0.7 copy.17
  101.2 0.7 copy.18
  101.9 0.7 copy.19
  102.6 0.6 copy.20
Async XLA Ops:
  1.3 1.7 %copy-start = (bf16[640,2048]{1,0:T(8,128)(2,1)S(1)}, bf16[640,2048]{1,0:T(8,128)(2,1)}, u32[]{:S(2)}) copy-start(bf16[640,2048]{1,0:T(8,128)(2,1)} %design.1) | copy-start | bytes 7864324
  3.1 1.1 %copy-start.1 = (bf16[1,640,640]{2,1,0:T(8,128)(2,1)S(1)}, bf16[1,640,640]{2,1,0:T(8,128)(2,1)}, u32[]{:S(2)}) copy-start(bf16[1,640,640]{2,1,0:T(8,128)(2,1)} %projector.1) | copy-start | bytes 2457604
  4.2 0.9 copy-start.2
  5.2 0.9 copy-start.3
  6.1 0.9 copy-start.4
  7.0 0.9 copy-start.5
  7.9 0.7 copy-start.6
  8.5 0.7 copy-start.7

commit v2 on v1

v2 whole, which is shorter than its diff:
```python
import functools

import jax
import jax.numpy as jnp
from jax import lax
from jax.experimental import pallas as pl
from jax.experimental.pallas import tpu as pltpu
from jax.sharding import PartitionSpec as P

ITERS = 5
MESH = pl.DeviceIdType.MESH
BF16 = jnp.bfloat16
F32 = jnp.float32


def shrink(values, threshold):
    return jnp.maximum(values - threshold, 0.0) - jnp.maximum(-values - threshold, 0.0)


def times(left, right):
    return jnp.dot(left, right, preferred_element_type=F32)


def times_transpose(left, right):
    return lax.dot_general(left, right, (((1,), (1,)), ((), ())), preferred_element_type=F32)


def kernel(
    rows, cols, split,
    design, projector, targets, sparsity, ridge, coefficients, block_duals, row_duals, block_fits,
    o_z, o_xc, o_xd, o_yd,
    A, K, S, XD, PX, AV, XB, PY, FIT, YD, YR, U, THR, SHR, XC, HC, R, Q,
    load_a, load_k, load_v, load_x, load_z, store,
    r_send, r_recv, q_send, q_recv, a_send, a_recv, b_send, b_recv, p_send, p_recv,
):
    blocks, size, width = S.shape
    part = size // split
    me_row, me_col = lax.axis_index("row"), lax.axis_index("col")

    def partner(k):
        other, bit = me_row, 1
        while bit < rows:
            if k & bit:
                other = other + bit * (1 - 2 * ((me_row // bit) % 2))
            bit *= 2
        return other

    def beside(k):
        return {"col": lax.rem(me_col + k, cols)}

    def block_of(p):
        return p // split

    def piece(ref, p):
        if split == 1:
            return ref.at[p]
        return ref.at[p // split, pl.ds(pl.multiple_of((p % split) * part, part), part), :]

    def remote(src, dst, send, recv, device):
        return pltpu.make_async_remote_copy(
            src_ref=src, dst_ref=dst, send_sem=send, recv_sem=recv, device_id=device, device_id_type=MESH)

    def columns(c):
        return pl.ds(c * width, width)

    near = list(range(1, rows))
    far = near[::-1]

    barrier = pltpu.get_barrier_semaphore()
    peers = [{"row": partner(k)} for k in near] + [beside(k) for k in range(1, cols)]
    for peer in peers:
        pl.semaphore_signal(barrier, inc=1, device_id=peer, device_id_type=MESH)

    load_xd = [pltpu.make_async_copy(block_duals.at[0, :, columns(c)], XD.at[c], load_x.at[c]) for c in range(blocks)]
    load_fit = pltpu.make_async_copy(block_fits.at[0], FIT, load_v.at[0])
    load_yd = pltpu.make_async_copy(row_duals, YD, load_v.at[1])
    load_zs = [pltpu.make_async_copy(coefficients.at[:, columns(c)], AV.at[c], load_z.at[c]) for c in range(blocks)]
    load_as = [pltpu.make_async_copy(design.at[:, columns(c)], A.at[c], load_a.at[c]) for c in range(blocks)]
    load_kk = pltpu.make_async_copy(projector.at[0], K, load_k.at[0])
    load_fit.start()
    load_yd.start()
    for copy in load_xd:
        copy.start()
    for c in range(blocks):
        load_as[c].start()
        load_zs[c].start()
    load_kk.start()

    eye = lax.broadcasted_iota(jnp.int32, (size, size), 0) == lax.broadcasted_iota(jnp.int32, (size, size), 1)

    def upright(ref):
        return jnp.sum(jnp.where(eye, ref[...], 0.0), axis=1, keepdims=True)

    THR[...] = jnp.broadcast_to(upright(sparsity), (size, width))
    SHR[...] = jnp.broadcast_to(1.0 / (1.0 + upright(ridge)), (size, width))

    pl.semaphore_wait(barrier, len(peers))

    def share(ref, slots, send, recv, k):
        return remote(piece(ref, partner(k)), slots.at[k - 1], send.at[k - 1], recv.at[k - 1], {"row": partner(k)})

    def spread(ref, send, recv, k):
        mine = piece(ref, me_row)
        return remote(mine, mine, send.at[k - 1], recv.at[k - 1], {"row": partner(k)})

    def take(ref, send, recv, k):
        other = piece(ref, partner(k))
        remote(other, other, send.at[k - 1], recv.at[k - 1], {"row": partner(k)}).wait_recv()

    def send_fit(slot, k):
        return remote(PY.at[slot, me_col], PY.at[slot, me_col], p_send.at[slot, k - 1], p_recv.at[slot, k - 1], beside(k))

    def take_fit(slot, k):
        source = lax.rem(me_col + cols - k, cols)
        remote(PY.at[slot, source], PY.at[slot, source], p_send.at[slot, k - 1], p_recv.at[slot, k - 1], beside(k)).wait_recv()

    def sum_fit(slot):
        total = PY[slot, 0]
        for j in range(1, cols):
            total = total + PY[slot, j]
        return total

    load_fit.wait()
    load_yd.wait()
    PY[2, me_col] = FIT[...]
    for k in range(1, cols):
        send_fit(2, k).start()
    for copy in load_xd:
        copy.wait()
    for k in far:
        share(XD, Q, q_send, q_recv, k).start()

    lifted = (FIT[...] + YD[...]).astype(BF16)
    total_u = None
    for c in range(blocks):
        load_as[c].wait()
        load_zs[c].wait()
        s = AV[c] - XD[c] + times(lifted, A[c])
        S[c] = s
        u = times_transpose(s.astype(BF16), A[c])
        total_u = u if total_u is None else total_u + u
    U[...] = total_u
    load_kk.wait()

    def project(slot):
        w = times(U[...].astype(BF16), K[...]).astype(BF16)
        for k in far + [0]:
            if split == 1 or k % split == split - 1:
                c = block_of(partner(k))
                PX[c] = S[c] - times(w, A[c])
            if k:
                share(PX, R, r_send, r_recv, k).start()
        block_y = None
        for c in range(blocks):
            y = times_transpose(PX[c].astype(BF16), A[c])
            block_y = y if block_y is None else block_y + y
        PY[slot, me_col] = block_y
        for k in range(1, cols):
            send_fit(slot, k).start()

    my_rows = pl.ds(pl.multiple_of((me_row % split) * part, part), part)

    def half_col():
        return shrink(piece(AV, me_row)[...] - XC[...], THR[my_rows, :]) * SHR[my_rows, :]

    def sum_shares(ref, slots, send, recv):
        total = piece(ref, me_row)[...]
        for k in near:
            share(ref, slots, send, recv, k).wait_recv()
            total = total + slots[k - 1]
        return total

    def average():
        avg = (HC[...] + sum_shares(PX, R, r_send, r_recv)) / (rows + 1)
        piece(AV, me_row)[...] = avg
        for k in far:
            spread(AV, a_send, a_recv, k).start()
        return avg

    def row_update(slot):
        half_row = 0.5 * (YR[...] - YD[...] + targets[...])
        for k in range(1, cols):
            take_fit(slot, k)
        misfit = (half_row - sum_fit(slot)) / (cols + 1)
        YR[...] = half_row - misfit
        YD[...] = YD[...] + misfit
        return misfit

    def settle(slot):
        for k in near:
            share(PX, R, r_send, r_recv, k).wait_send()
            spread(AV, a_send, a_recv, k).wait_send()
        for k in range(1, cols):
            send_fit(slot, k).wait_send()

    project(0)

    XC[...] = -sum_shares(XD, Q, q_send, q_recv)
    HC[...] = half_col()
    for k in range(1, cols):
        take_fit(2, k)
    YR[...] = sum_fit(2)
    for k in range(1, cols):
        send_fit(2, k).wait_send()
    for k in near:
        share(XD, Q, q_send, q_recv, k).wait_send()

    def step(t, carry):
        slot = lax.rem(t, 2)
        avg = average()
        XC[...] = XC[...] + HC[...] - avg
        HC[...] = half_col()
        misfit = row_update(slot)
        lifted = (PY[slot, me_col] + misfit + YD[...]).astype(BF16)
        for c in range(blocks):
            S[c] = times(lifted, A[c])
        total_u = jnp.zeros(U.shape, F32)
        for k in [0] + near:
            if k:
                take(AV, a_send, a_recv, k)
            if split == 1 or k % split == split - 1:
                c = block_of(partner(k))
                duals = XD[c] + PX[c] - AV[c]
                XD[c] = duals
                s = AV[c] - duals + S[c]
                S[c] = s
                total_u = total_u + times_transpose(s.astype(BF16), A[c])
        U[...] = total_u
        settle(slot)
        project(1 - slot)
        return carry

    lax.fori_loop(0, ITERS - 1, step, 0)

    slot = (ITERS - 1) % 2
    piece(XB, me_row)[...] = XC[...] + HC[...]
    for k in far:
        spread(XB, b_send, b_recv, k).start()
    average()
    row_update(slot)
    stores = [pltpu.make_async_copy(YD, o_yd, store.at[0, 0])]
    stores[0].start()
    for k in near:
        spread(XB, b_send, b_recv, k).wait_send()
    for k in [0] + near:
        if k:
            take(XB, b_send, b_recv, k)
            take(AV, a_send, a_recv, k)
        if split == 1 or k % split == split - 1:
            c = block_of(partner(k))
            where = pl.ds(pl.multiple_of(c * width, width), width)
            XD[c] = XD[c] + PX[c] - AV[c]
            XB[c] = XB[c] - AV[c]
            n = len(stores)
            for ref, out in ((AV, o_z), (XB, o_xc), (XD, o_xd.at[0])):
                copy = pltpu.make_async_copy(ref.at[c], out.at[:, where], store.at[n, len(stores) - n])
                copy.start()
                stores.append(copy)
    settle(slot)
    for copy in stores:
        copy.wait()


def per_device(design, projector, targets, sparsity, ridge_weight, coefficients, block_duals, row_duals, block_fits):
    rows, cols = lax.axis_size("row"), lax.axis_size("col")
    size, n = coefficients.shape
    m = design.shape[0]
    width = max(128, n // rows)
    blocks = n // width
    split = rows // blocks
    part = size // split
    any_space = pl.BlockSpec(memory_space=pl.ANY)
    vmem = pl.BlockSpec(memory_space=pltpu.VMEM)
    dma = pltpu.SemaphoreType.DMA
    wide = pltpu.VMEM((blocks, size, width), F32)
    tall = pltpu.VMEM((size, m), F32)
    own = pltpu.VMEM((part, width), F32)
    slots = pltpu.VMEM((rows - 1, part, width), F32)
    scratch = [
        pltpu.VMEM((blocks, m, width), BF16), pltpu.VMEM((m, m), BF16),
        wide, wide, wide, wide, wide,
        pltpu.VMEM((3, cols, size, m), F32), tall, tall, tall, tall,
        pltpu.VMEM((size, width), F32), pltpu.VMEM((size, width), F32), own, own,
        slots, slots,
        dma((blocks,)), dma((1,)), dma((2,)), dma((blocks,)), dma((blocks,)), dma((3 * blocks + 1, 3)),
        dma((rows - 1,)), dma((rows - 1,)), dma((rows - 1,)), dma((rows - 1,)),
        dma((rows - 1,)), dma((rows - 1,)), dma((rows - 1,)), dma((rows - 1,)),
        dma((3, cols - 1)), dma((3, cols - 1)),
    ]
    return pl.pallas_call(
        functools.partial(kernel, rows, cols, split),
        out_shape=(
            jax.ShapeDtypeStruct((size, n), F32),
            jax.ShapeDtypeStruct((size, n), F32),
            jax.ShapeDtypeStruct((1, size, n), F32),
            jax.ShapeDtypeStruct((size, m), F32),
        ),
        in_specs=[any_space, any_space, vmem, vmem, vmem, any_space, any_space, any_space, any_space],
        out_specs=[any_space] * 4,
        scratch_shapes=scratch,
        compiler_params=pltpu.CompilerParams(
            collective_id=0, has_side_effects=True, vmem_limit_bytes=60 * 1024 * 1024),
        name="admm",
    )(design, projector, targets.reshape(1, m), sparsity.reshape(1, size), ridge_weight.reshape(1, size),
      coefficients, block_duals, row_duals, block_fits)


def solution(mesh):
    return jax.shard_map(
        per_device,
        mesh=mesh,
        in_specs=(
            P("row", "col"),
            P("col", "row", None),
            P("row"),
            P(),
            P(),
            P(None, "col"),
            P("row", None, "col"),
            P(None, "row"),
            P("col", None, "row"),
        ),
        out_specs=(P(None, "col"), P(None, "col"), P("row", None, "col"), P(None, "row")),
        check_vma=False,
    )
```

time: 104 us -> 95.9 us (0.922)
  Pallas kernels: 91.3 us -> 87.2 us
  local copies, waits for them, and re-layouts: 11.3 us -> 7.8 us
    pallas_call x1, Pallas kernels: 91.3 us -> 87.2 us  [per_device(): pl.pallas_call(functools.partial(kernel, rows, cols, split), out_shape=(j...]
    unnamed x20 -> x4, local copies, waits for them, and re-layouts: 10.6 us -> 6.53 us
where the time goes in v2:
time: 95.9 us; the launch traced here: 95.6 us
  Pallas kernels  87.2 us (91%)
  local copies, waits for them, and re-layouts  7.8 us (8%)
    pallas_call x1, Pallas kernels, per_device(): pl.pallas_call(functools.partial(kernel, rows, cols, split), out_shape=(j...  87.2 us
    unnamed x4, local copies, waits for them, and re-layouts  6.53 us

profile of v2, /device:TPU:0, one launch (start us, length us, event | category | flops | bytes accessed | tf_op | source)
XLA Modules:
  0.0 95.6 jit_solution(3235966480682969388)
XLA Ops:
  0.6 1.3 %reshape.17.targets = f32[1,640]{1,0:T(1,128)} reshape(f32[640]{0:T(1024)} %param.11) | data formatting | bytes 5120 | tf_op jit(solution)/shard_map/reshape | solution.py:304
  1.9 87.2 %admm.1 = (f32[32,2048]{1,0:T(8,128)}, f32[32,2048]{1,0:T(8,128)}, f32[1,32,2048]{2,1,0:T(8,128)}, f32[32,640]{1,0:T(8,128)}) custom-call(bf16[640,2048]{1,0:T(8,128)(2,1)} %design.1, bf16[1,640,640]{2,1,0:T(8,128)(2,1)} %projector.1, f32[1,640]{1,0:T(1,128)} %reshape.17.targets, f32[1,32]{1,0:T(1,128)} %bitcast.2, f32[1,32]{1,0:T(1,128)} %bitcast.3, ...), custom_call_target="tpu_custom_call" | custom-call | tf_op jit(solution)/shard_map/admm/pallas_call | solution.py:290
  89.1 1.7 %copy.17 = f32[32,2048]{1,0:T(8,128)} copy(f32[32,2048]{1,0:T(8,128)} %get-tuple-element.8) | data formatting | bytes 524288
  90.7 1.7 %copy.18 = f32[32,2048]{1,0:T(8,128)} copy(f32[32,2048]{1,0:T(8,128)} %get-tuple-element.9) | data formatting | bytes 524288
  92.4 1.7 %copy.19 = f32[1,32,2048]{2,1,0:T(8,128)} copy(f32[1,32,2048]{2,1,0:T(8,128)} %get-tuple-element.10) | data formatting | bytes 524288
  94.1 1.5 %copy.20 = f32[32,640]{1,0:T(8,128)} copy(f32[32,640]{1,0:T(8,128)} %get-tuple-element.11) | data formatting | bytes 163840

commit v3 on v0

v3 whole, which is shorter than its diff:
```python
import functools

import jax
import jax.numpy as jnp
from jax import lax
from jax.experimental import pallas as pl
from jax.experimental.pallas import tpu as pltpu
from jax.sharding import PartitionSpec as P

ITERS = 5
MESH = pl.DeviceIdType.MESH
BF16 = jnp.bfloat16
F32 = jnp.float32


def shrink(values, threshold):
    return jnp.maximum(values - threshold, 0.0) - jnp.maximum(-values - threshold, 0.0)


def times(left, right):
    return jnp.dot(left, right, preferred_element_type=F32)


def times_transpose(left, right):
    return lax.dot_general(left, right, (((1,), (1,)), ((), ())), preferred_element_type=F32)


HALVES = 2


def kernel(
    rows, cols, split,
    design, projector, targets, sparsity, ridge, coefficients, block_duals, row_duals, block_fits,
    o_z, o_xc, o_xd, o_yd,
    A, K, S, XD, PX, AV, XB, PY, FIT, YD, YR, U, THR, SHR, XC, HC, R, Q,
    load_a, load_k, load_v, load_x, load_z, store,
    r_send, r_recv, q_send, q_recv, a_send, a_recv, b_send, b_recv, p_send, p_recv,
):
    blocks, size, width = S.shape[1:]
    part = size // split
    me_row, me_col = lax.axis_index("row"), lax.axis_index("col")
    halves = range(HALVES)

    def partner(k):
        other, bit = me_row, 1
        while bit < rows:
            if k & bit:
                other = other + bit * (1 - 2 * ((me_row // bit) % 2))
            bit *= 2
        return other

    def beside(k):
        return {"col": lax.rem(me_col + k, cols)}

    def block_of(p):
        return p // split

    def piece(ref, h, p):
        if split == 1:
            return ref.at[h, p]
        return ref.at[h, p // split, pl.ds(pl.multiple_of((p % split) * part, part), part), :]

    def remote(src, dst, send, recv, device):
        return pltpu.make_async_remote_copy(
            src_ref=src, dst_ref=dst, send_sem=send, recv_sem=recv, device_id=device, device_id_type=MESH)

    def columns(c):
        return pl.ds(c * width, width)

    def group(h):
        return pl.ds(h * size, size)

    near = list(range(1, rows))
    far = near[::-1]

    barrier = pltpu.get_barrier_semaphore()
    peers = [{"row": partner(k)} for k in near] + [beside(k) for k in range(1, cols)]
    for peer in peers:
        pl.semaphore_signal(barrier, inc=1, device_id=peer, device_id_type=MESH)

    load_fit = [pltpu.make_async_copy(block_fits.at[0, group(h), :], FIT.at[h], load_v.at[0, h]) for h in halves]
    load_yd = [pltpu.make_async_copy(row_duals.at[group(h), :], YD.at[h], load_v.at[1, h]) for h in halves]
    load_xd = [[pltpu.make_async_copy(block_duals.at[0, group(h), columns(c)], XD.at[h, c], load_x.at[h, c])
                for c in range(blocks)] for h in halves]
    load_zs = [[pltpu.make_async_copy(coefficients.at[group(h), columns(c)], AV.at[h, c], load_z.at[h, c])
                for c in range(blocks)] for h in halves]
    load_as = [pltpu.make_async_copy(design.at[:, columns(c)], A.at[c], load_a.at[c]) for c in range(blocks)]
    load_kk = pltpu.make_async_copy(projector.at[0], K, load_k.at[0])
    for h in halves:
        load_fit[h].start()
        load_yd[h].start()
        for copy in load_xd[h]:
            copy.start()
    for c in range(blocks):
        load_as[c].start()
        load_zs[0][c].start()
    load_kk.start()
    for c in range(blocks):
        load_zs[1][c].start()

    eye = lax.broadcasted_iota(jnp.int32, (size, size), 0) == lax.broadcasted_iota(jnp.int32, (size, size), 1)

    def upright(ref, h):
        return jnp.sum(jnp.where(eye, ref[:, h * size:(h + 1) * size], 0.0), axis=1, keepdims=True)

    for h in halves:
        THR[h] = jnp.broadcast_to(upright(sparsity, h), (size, width))
        SHR[h] = jnp.broadcast_to(1.0 / (1.0 + upright(ridge, h)), (size, width))

    pl.semaphore_wait(barrier, len(peers))

    def share(ref, slots, send, recv, h, k):
        return remote(
            piece(ref, h, partner(k)), slots.at[h, k - 1], send.at[h, k - 1], recv.at[h, k - 1], {"row": partner(k)})

    def spread(ref, send, recv, h, k):
        mine = piece(ref, h, me_row)
        return remote(mine, mine, send.at[h, k - 1], recv.at[h, k - 1], {"row": partner(k)})

    def take(ref, send, recv, h, k):
        other = piece(ref, h, partner(k))
        remote(other, other, send.at[h, k - 1], recv.at[h, k - 1], {"row": partner(k)}).wait_recv()

    def fit_copy(slot, h, source, k):
        own = PY.at[slot, h, source]
        return remote(own, own, p_send.at[slot, h, k - 1], p_recv.at[slot, h, k - 1], beside(k))

    def send_fit(slot, h, k):
        return fit_copy(slot, h, me_col, k)

    def sum_fit(slot, h):
        for k in range(1, cols):
            fit_copy(slot, h, lax.rem(me_col + cols - k, cols), k).wait_recv()
        total = PY[slot, h, 0]
        for j in range(1, cols):
            total = total + PY[slot, h, j]
        return total

    for h in halves:
        load_fit[h].wait()
        load_yd[h].wait()
        PY[2, h, me_col] = FIT[h]
        for k in range(1, cols):
            send_fit(2, h, k).start()
    for h in halves:
        for copy in load_xd[h]:
            copy.wait()
        for k in far:
            share(XD, Q, q_send, q_recv, h, k).start()

    def begin(h):
        lifted = (FIT[h] + YD[h]).astype(BF16)
        total_u = None
        for c in range(blocks):
            if h == 0:
                load_as[c].wait()
            load_zs[h][c].wait()
            s = AV[h, c] - XD[h, c] + times(lifted, A[c])
            S[h, c] = s
            u = times_transpose(s.astype(BF16), A[c])
            total_u = u if total_u is None else total_u + u
        U[h] = total_u
        if h == 0:
            load_kk.wait()

    def project_x(h):
        w = times(U[h].astype(BF16), K[...]).astype(BF16)
        for k in far + [0]:
            if split == 1 or k % split == split - 1:
                c = block_of(partner(k))
                PX[h, c] = S[h, c] - times(w, A[c])
            if k:
                share(PX, R, r_send, r_recv, h, k).start()

    def project_y(h, slot):
        block_y = None
        for c in range(blocks):
            y = times_transpose(PX[h, c].astype(BF16), A[c])
            block_y = y if block_y is None else block_y + y
        PY[slot, h, me_col] = block_y
        for k in range(1, cols):
            send_fit(slot, h, k).start()

    my_rows = pl.ds(pl.multiple_of((me_row % split) * part, part), part)

    def half_col(h):
        return shrink(piece(AV, h, me_row)[...] - XC[h], THR[h, my_rows, :]) * SHR[h, my_rows, :]

    def sum_shares(ref, slots, send, recv, h):
        total = piece(ref, h, me_row)[...]
        for k in near:
            share(ref, slots, send, recv, h, k).wait_recv()
            total = total + slots[h, k - 1]
        return total

    def average(h):
        avg = (HC[h] + sum_shares(PX, R, r_send, r_recv, h)) / (rows + 1)
        piece(AV, h, me_row)[...] = avg
        for k in far:
            spread(AV, a_send, a_recv, h, k).start()
        XC[h] = XC[h] + HC[h] - avg
        HC[h] = half_col(h)

    def row_update(h, slot):
        half_row = 0.5 * (YR[h] - YD[h] + targets[...])
        misfit = (half_row - sum_fit(slot, h)) / (cols + 1)
        YR[h] = half_row - misfit
        YD[h] = YD[h] + misfit
        return misfit

    def lift(h, slot):
        misfit = row_update(h, slot)
        lifted = (PY[slot, h, me_col] + misfit + YD[h]).astype(BF16)
        for c in range(blocks):
            S[h, c] = times(lifted, A[c])

    def gather(h):
        total_u = jnp.zeros(U.shape[1:], F32)
        for k in [0] + near:
            if k:
                take(AV, a_send, a_recv, h, k)
            if split == 1 or k % split == split - 1:
                c = block_of(partner(k))
                duals = XD[h, c] + PX[h, c] - AV[h, c]
                XD[h, c] = duals
                s = AV[h, c] - duals + S[h, c]
                S[h, c] = s
                total_u = total_u + times_transpose(s.astype(BF16), A[c])
        U[h] = total_u

    def settle(h, slot):
        for k in near:
            share(PX, R, r_send, r_recv, h, k).wait_send()
            spread(AV, a_send, a_recv, h, k).wait_send()
        for k in range(1, cols):
            send_fit(slot, h, k).wait_send()

    for h in halves:
        begin(h)
        project_x(h)
    for h in halves:
        project_y(h, 0)

    for h in halves:
        XC[h] = -sum_shares(XD, Q, q_send, q_recv, h)
        HC[h] = half_col(h)
        YR[h] = sum_fit(2, h)
        for k in range(1, cols):
            send_fit(2, h, k).wait_send()
        for k in near:
            share(XD, Q, q_send, q_recv, h, k).wait_send()
        if h == 0:
            average(0)
    lift(0, 0)

    def step(t, carry):
        slot = lax.rem(t, 2)
        gather(0)
        settle(0, slot)
        project_x(0)
        average(1)
        project_y(0, 1 - slot)
        lift(1, slot)
        average(0)
        gather(1)
        settle(1, slot)
        project_x(1)
        project_y(1, 1 - slot)
        lift(0, 1 - slot)
        return carry

    lax.fori_loop(0, ITERS - 1, step, 0)

    slot = (ITERS - 1) % 2
    piece(XB, 0, me_row)[...] = XC[0]
    piece(XB, 1, me_row)[...] = XC[1] + HC[1]
    for h in (1, 0):
        for k in far:
            spread(XB, b_send, b_recv, h, k).start()
    average(1)
    row_update(1, slot)
    stores = [pltpu.make_async_copy(YD.at[h], o_yd.at[group(h), :], store.at[0, h]) for h in halves]
    for copy in stores:
        copy.start()
    for h in halves:
        for k in near:
            spread(XB, b_send, b_recv, h, k).wait_send()
        done = 1
        for k in [0] + near:
            if k:
                take(AV, a_send, a_recv, h, k)
                take(XB, b_send, b_recv, h, k)
            if split == 1 or k % split == split - 1:
                c = block_of(partner(k))
                where = pl.ds(pl.multiple_of(c * width, width), width)
                XD[h, c] = XD[h, c] + PX[h, c] - AV[h, c]
                if h == 1:
                    XB[h, c] = XB[h, c] - AV[h, c]
                for ref, out in ((AV, o_z), (XB, o_xc), (XD, o_xd.at[0])):
                    copy = pltpu.make_async_copy(ref.at[h, c], out.at[group(h), where], store.at[done, h])
                    copy.start()
                    stores.append(copy)
                    done += 1
    for h in halves:
        settle(h, slot)
    for copy in stores:
        copy.wait()


def hand_over(*refs):
    count = len(refs) // 2
    sems = refs[-1]
    copies = [pltpu.make_async_copy(refs[i], refs[count + i], sems.at[i]) for i in range(count)]
    for copy in copies:
        copy.start()
    for copy in copies:
        copy.wait()


def per_device(design, projector, targets, sparsity, ridge_weight, coefficients, block_duals, row_duals, block_fits):
    rows, cols = lax.axis_size("row"), lax.axis_size("col")
    total, n = coefficients.shape
    m = design.shape[0]
    size = total // HALVES
    width = max(128, n // rows)
    blocks = n // width
    split = rows // blocks
    part = size // split
    any_space = pl.BlockSpec(memory_space=pl.ANY)
    vmem = pl.BlockSpec(memory_space=pltpu.VMEM)
    dma = pltpu.SemaphoreType.DMA
    wide = pltpu.VMEM((HALVES, blocks, size, width), F32)
    tall = pltpu.VMEM((HALVES, size, m), F32)
    own = pltpu.VMEM((HALVES, part, width), F32)
    full = pltpu.VMEM((HALVES, size, width), F32)
    slots = pltpu.VMEM((HALVES, rows - 1, part, width), F32)
    scratch = [
        pltpu.VMEM((blocks, m, width), BF16), pltpu.VMEM((m, m), BF16),
        wide, wide, wide, wide, wide,
        pltpu.VMEM((3, HALVES, cols, size, m), F32), tall, tall, tall, tall,
        full, full, own, own, slots, slots,
        dma((blocks,)), dma((1,)), dma((2, HALVES)), dma((HALVES, blocks)), dma((HALVES, blocks)),
        dma((3 * blocks + 1, HALVES)),
    ] + [dma((HALVES, rows - 1))] * 8 + [dma((3, HALVES, cols - 1))] * 2
    shapes = (
        jax.ShapeDtypeStruct((total, n), F32),
        jax.ShapeDtypeStruct((total, n), F32),
        jax.ShapeDtypeStruct((1, total, n), F32),
        jax.ShapeDtypeStruct((total, m), F32),
    )
    results = pl.pallas_call(
        functools.partial(kernel, rows, cols, split),
        out_shape=shapes,
        in_specs=[any_space, any_space, vmem, vmem, vmem, any_space, any_space, any_space, any_space],
        out_specs=[any_space] * 4,
        scratch_shapes=scratch,
        compiler_params=pltpu.CompilerParams(
            collective_id=0, has_side_effects=True, vmem_limit_bytes=60 * 1024 * 1024),
        name="admm",
    )(design, projector, targets.reshape(1, m), sparsity.reshape(1, total), ridge_weight.reshape(1, total),
      coefficients, block_duals, row_duals, block_fits)
    return pl.pallas_call(
        hand_over,
        out_shape=shapes,
        in_specs=[any_space] * 4,
        out_specs=[any_space] * 4,
        scratch_shapes=[dma((4,))],
        compiler_params=pltpu.CompilerParams(vmem_limit_bytes=60 * 1024 * 1024),
        name="hand_over",
    )(*results)


def solution(mesh):
    return jax.shard_map(
        per_device,
        mesh=mesh,
        in_specs=(
            P("row", "col"),
            P("col", "row", None),
            P("row"),
            P(),
            P(),
            P(None, "col"),
            P("row", None, "col"),
            P(None, "row"),
            P("col", None, "row"),
        ),
        out_specs=(P(None, "col"), P(None, "col"), P("row", None, "col"), P(None, "row")),
        check_vma=False,
    )
```

time: 590 us -> 114 us (0.19)
  waiting for transfers between devices: 511 us -> 0 us
  Pallas kernels: 0 us -> 112 us
  matrix products: 46.1 us -> 0 us
  other arithmetic: 15.2 us -> 0 us
  between operations: 14.3 us -> 0.64 us
    psum x10 -> x0, waiting for transfers between devices: 509 us -> none  [the longest x5 356 us: per_device(): total = lax.psum(block_x, 'row')]
    pallas_call x0 -> x2, Pallas kernels: none -> 112 us  [the longest x1 84.9 us: per_device(): pl.pallas_call(functools.partial(kernel, rows, cols, split), out_shape=sh...]
    dot_general x20 -> x0, matrix products: 46.1 us -> none  [the longest x5 13.4 us: per_device(): jnp.dot(image.astype(jnp.bfloat16), inverse, preferred_element_type=jnp.f...]
    sub x3 -> x0, other arithmetic: 7.06 us -> none  [the longest x2 4.99 us: per_device(): shares = shares + block_x - average]
  transfers between devices with their start and end apart: 10 -> 0, of which waited for: 10 -> 0; matrix products, arithmetic and copies ran while one was open for 3% -> 0% of each run, Pallas kernels for 0% -> 0%
where the time goes in v3:
time: 114 us
  Pallas kernels  112 us (98%)
  local copies, waits for them, and re-layouts  1.27 us (1%)
    pallas_call x1, Pallas kernels, per_device(): pl.pallas_call(functools.partial(kernel, rows, cols, split), out_shape=sh...  84.9 us
    pallas_call x1, Pallas kernels, per_device(): pl.pallas_call(hand_over, out_shape=shapes, in_specs=[any_space] * 4, out...  27.4 us

profile of v3, /device:TPU:0, one launch (start us, length us, event | category | flops | bytes accessed | tf_op | source)
XLA Modules:
  0.0 114.3 jit_solution(16390869327546575483)
XLA Ops:
  0.6 1.3 %reshape.17.targets = f32[1,640]{1,0:T(1,128)} reshape(f32[640]{0:T(1024)} %param.11) | data formatting | bytes 5120 | tf_op jit(solution)/shard_map/reshape | solution.py:360
  1.9 84.9 %admm.1 = (f32[32,2048]{1,0:T(8,128)}, f32[32,2048]{1,0:T(8,128)}, f32[1,32,2048]{2,1,0:T(8,128)}, f32[32,640]{1,0:T(8,128)}) custom-call(bf16[640,2048]{1,0:T(8,128)(2,1)} %design.1, bf16[1,640,640]{2,1,0:T(8,128)(2,1)} %projector.1, f32[1,640]{1,0:T(1,128)} %reshape.17.targets, f32[1,32]{1,0:T(1,128)} %bitcast.2, f32[1,32]{1,0:T(1,128)} %bitcast.3, ...), custom_call_target="tpu_custom_call" | custom-call | tf_op jit(solution)/shard_map/admm/pallas_call | solution.py:351
  86.8 27.4 %hand_over.1 = (f32[32,2048]{1,0:T(8,128)}, f32[32,2048]{1,0:T(8,128)}, f32[1,32,2048]{2,1,0:T(8,128)}, f32[32,640]{1,0:T(8,128)}) custom-call(f32[32,2048]{1,0:T(8,128)} %get-tuple-element.8.refs_0_, f32[32,2048]{1,0:T(8,128)} %get-tuple-element.9.refs_1_, f32[1,32,2048]{2,1,0:T(8,128)} %get-tuple-element.10.refs_2_, f32[32,640]{1,0:T(8,128)} %get-tuple-element.11.refs_3_), custom_call_target="tpu_custom_call" | custom-call | tf_op jit(solution)/shard_map/hand_over/pallas_call | solution.py:362

commit v4 on v3

--- a/solution.py
+++ b/solution.py
@@ -202,7 +202,7 @@
         HC[h] = half_col(h)
 
     def row_update(h, slot):
-        half_row = 0.5 * (YR[h] - YD[h] + targets[...])
+        half_row = 0.5 * (YR[h] - YD[h] + targets[...].reshape(1, -1))
         misfit = (half_row - sum_fit(slot, h)) / (cols + 1)
         YR[h] = half_row - misfit
         YD[h] = YD[h] + misfit
@@ -307,16 +307,6 @@
         copy.wait()
 
 
-def hand_over(*refs):
-    count = len(refs) // 2
-    sems = refs[-1]
-    copies = [pltpu.make_async_copy(refs[i], refs[count + i], sems.at[i]) for i in range(count)]
-    for copy in copies:
-        copy.start()
-    for copy in copies:
-        copy.wait()
-
-
 def per_device(design, projector, targets, sparsity, ridge_weight, coefficients, block_duals, row_duals, block_fits):
     rows, cols = lax.axis_size("row"), lax.axis_size("col")
     total, n = coefficients.shape
@@ -327,6 +317,7 @@
     split = rows // blocks
     part = size // split
     any_space = pl.BlockSpec(memory_space=pl.ANY)
+    hbm = pl.BlockSpec(memory_space=pltpu.HBM)
     vmem = pl.BlockSpec(memory_space=pltpu.VMEM)
     dma = pltpu.SemaphoreType.DMA
     wide = pltpu.VMEM((HALVES, blocks, size, width), F32)
@@ -343,31 +334,22 @@
         dma((3 * blocks + 1, HALVES)),
     ] + [dma((HALVES, rows - 1))] * 8 + [dma((3, HALVES, cols - 1))] * 2
     shapes = (
-        jax.ShapeDtypeStruct((total, n), F32),
-        jax.ShapeDtypeStruct((total, n), F32),
-        jax.ShapeDtypeStruct((1, total, n), F32),
-        jax.ShapeDtypeStruct((total, m), F32),
+        pltpu.VMEM((total, n), F32),
+        pltpu.VMEM((total, n), F32),
+        pltpu.VMEM((1, total, n), F32),
+        pltpu.VMEM((total, m), F32),
     )
-    results = pl.pallas_call(
+    return pl.pallas_call(
         functools.partial(kernel, rows, cols, split),
         out_shape=shapes,
-        in_specs=[any_space, any_space, vmem, vmem, vmem, any_space, any_space, any_space, any_space],
-        out_specs=[any_space] * 4,
+        in_specs=[hbm, hbm, vmem, vmem, vmem, hbm, hbm, hbm, hbm],
+        out_specs=[vmem] * 4,
         scratch_shapes=scratch,
         compiler_params=pltpu.CompilerParams(
-            collective_id=0, has_side_effects=True, vmem_limit_bytes=60 * 1024 * 1024),
+            collective_id=0, has_side_effects=True, vmem_limit_bytes=59 * 1024 * 1024),
         name="admm",
-    )(design, projector, targets.reshape(1, m), sparsity.reshape(1, total), ridge_weight.reshape(1, total),
+    )(design, projector, targets, sparsity.reshape(1, total), ridge_weight.reshape(1, total),
       coefficients, block_duals, row_duals, block_fits)
-    return pl.pallas_call(
-        hand_over,
-        out_shape=shapes,
-        in_specs=[any_space] * 4,
-        out_specs=[any_space] * 4,
-        scratch_shapes=[dma((4,))],
-        compiler_params=pltpu.CompilerParams(vmem_limit_bytes=60 * 1024 * 1024),
-        name="hand_over",
-    )(*results)
 
 
 def solution(mesh):

time: 114 us -> 88.4 us (0.78)
  Pallas kernels: 112 us -> 84.9 us
  local copies, waits for them, and re-layouts: 1.27 us -> 2.74 us
    pallas_call x1 -> x0, Pallas kernels: 27.4 us -> none  [per_device(): pl.pallas_call(hand_over, out_shape=shapes, in_specs=[any_space] * 4, out...]
    unnamed x0 -> x4, local copies, waits for them, and re-layouts: none -> 2.74 us
    reshape x1 -> x0, local copies, waits for them, and re-layouts: 1.27 us -> none  [per_device(): targets.reshape(1, m)]
where the time goes in v4:
time: 88.4 us; the launch traced here: 88.3 us
  Pallas kernels  84.9 us (96%)
  local copies, waits for them, and re-layouts  2.74 us (3%)
    pallas_call x1, Pallas kernels, per_device(): pl.pallas_call(functools.partial(kernel, rows, cols, split), out_shape=sh...  84.9 us
    unnamed x4, local copies, waits for them, and re-layouts  2.74 us

profile of v4, /device:TPU:0, one launch (start us, length us, event | category | flops | bytes accessed | tf_op | source)
XLA Modules:
  0.0 88.3 jit_solution(18102364133219094252)
XLA Ops:
  0.6 84.9 %admm.1 = (f32[32,2048]{1,0:T(8,128)S(1)}, f32[32,2048]{1,0:T(8,128)S(1)}, f32[1,32,2048]{2,1,0:T(8,128)S(1)}, f32[32,640]{1,0:T(8,128)S(1)}) custom-call(bf16[640,2048]{1,0:T(8,128)(2,1)} %design.1, bf16[1,640,640]{2,1,0:T(8,128)(2,1)} %projector.1, f32[640]{0:T(1024)} %targets.1, f32[1,32]{1,0:T(1,128)} %bitcast.2, f32[1,32]{1,0:T(1,128)} %bitcast.3, ...), custom_call_target="tpu_custom_call" | custom-call | tf_op jit(solution)/shard_map/admm/pallas_call | solution.py:342
  85.5 0.7 copy.17
  86.2 0.6 copy.20
  86.9 0.7 copy.18
  87.6 0.7 copy.19
